TPU v7x, 512 devices: a whole 4x4x16 slice. The times are simulated.
512 devices in a mesh: row: 32 (over z, core), col: 16 (over y, x).
Axes of the slice: x: 4, y: 4, z: 16, core: 2. Of those that a mesh axis runs over, the one named last changes fastest.
Arguments:
- pred_feat: bfloat16 [327680, 64], P('row'), may hold values from -6 to 6
- true_feat: bfloat16 [262144, 64], P('col'), may hold values from -6 to 6
- neighbors: int32 [2560, 16, 12], P('row', 'col'), may hold values from 0 to 127, as said below
- counts: int32 [2560, 16], P('row'), may hold values from 0 to 12, as said below
Outputs:
- pred_potential: float32 [327680], P('row')
- true_potential: float32 [262144], P('col')
Inputs may be any that keep to these rules, and one draw needn't show every extreme that they name: neighbors[b, s, k] indexes a block among the 128 ground-truth blocks of column shard s; entries at k >= counts[b, s] are ignored; the live entries of one list are distinct; every ground-truth block is named by some live entry. Each predicted block b has a first column shard h with counts[b, h] >= 1, may have live entries in shard h + 1 modulo 16, and has none in any other shard; of the blocks of one index of row exactly 80 / 16 have each column shard as their first, so at most 2 * 80 / 16 blocks of one index of row have live entries in one column shard.
All inputs are finite; a program needn't handle non-finite values.
Results may differ from a plain program's by a relative error of at most 0.0003.
Values sent between devices are 32-bit elements; how exact they have to be, the bound alone decides.
A program may use at most 64 MiB of HBM per device.

v0:
```python
import math

import jax
import jax.numpy as jnp
from jax import lax
from jax.sharding import PartitionSpec as P

BLOCK = 128
ITERS = 3


EPSILON = 0.02
NEGATIVE = -1e30


def pair_costs(pred_blocks, true_blocks, neighbor_ids):
    chosen = jnp.take(true_blocks, neighbor_ids, axis=0)
    pred_sq = jnp.sum(jnp.square(pred_blocks.astype(jnp.float32)), -1)
    true_sq = jnp.sum(jnp.square(true_blocks.astype(jnp.float32)), -1)
    cross = jnp.einsum("rpf,rkqf->rkpq", pred_blocks, chosen, preferred_element_type=jnp.float32)
    near_sq = jnp.take(true_sq, neighbor_ids, axis=0)
    return (pred_sq[:, None, :, None] + near_sq[:, :, None, :] - 2.0 * cross) / pred_blocks.shape[
        -1
    ]


def on_device(pred_feat, true_feat, neighbors, counts):
    width = pred_feat.shape[1]
    block = BLOCK
    row_blocks = pred_feat.shape[0] // block
    col_blocks = true_feat.shape[0] // block
    members_col = lax.axis_size("col")
    here = lax.axis_index("col")
    column = lax.dynamic_index_in_dim(counts, here, 1, keepdims=False)
    capacity = 2 * row_blocks // members_col
    picked = jnp.argsort((column <= 0).astype(jnp.int32), stable=True)[:capacity]
    pred_blocks = jnp.take(pred_feat.reshape(row_blocks, block, width), picked, axis=0)
    true_blocks = true_feat.reshape(col_blocks, block, width)
    neighbor_ids = jnp.take(neighbors[:, 0, :], picked, axis=0)
    live_count = jnp.take(column, picked, axis=0)
    slots = jnp.arange(neighbor_ids.shape[1], dtype=jnp.int32)
    live_pair = slots[None, :] < live_count[:, None]
    live = live_pair[:, :, None, None]
    owner = (
        (neighbor_ids[:, :, None] == jnp.arange(col_blocks, dtype=jnp.int32)[None, None, :])
        & live_pair[:, :, None]
    ).astype(jnp.float32)
    log_pred = -math.log(pred_feat.shape[0] * lax.axis_size("row"))
    log_true = -math.log(true_feat.shape[0] * members_col)

    def spread(values, fill):
        return jnp.full((row_blocks, block), fill, jnp.float32).at[picked].set(values)

    true_pot = jnp.zeros((col_blocks * block,), jnp.float32)
    pred_pot = jnp.zeros((row_blocks, block), jnp.float32)
    for step in range(ITERS):
        cost = pair_costs(pred_blocks, true_blocks, neighbor_ids)
        near = jnp.take(true_pot.reshape(col_blocks, block), neighbor_ids, axis=0)
        scores = jnp.where(live, (near[:, :, None, :] - cost) / EPSILON, NEGATIVE)
        local_top = jnp.max(scores, axis=(1, 3))
        top = lax.pmax(spread(local_top, NEGATIVE), "col")
        chosen = jnp.take(top, picked, axis=0)
        local_total = jnp.sum(
            jnp.where(live, jnp.exp(scores - chosen[:, None, :, None]), 0.0), axis=(1, 3)
        )
        total = lax.psum(spread(local_total, 0.0), "col")
        positive = total > 0
        pred_pot = jnp.where(
            positive, EPSILON * (log_pred - top - jnp.log(jnp.where(positive, total, 1.0))), 0.0
        )
        near_pred = jnp.take(pred_pot, picked, axis=0)
        col_scores = jnp.where(live, (near_pred[:, None, :, None] - cost) / EPSILON, NEGATIVE)
        pair_top = jnp.max(col_scores, axis=2)
        local_col_top = jnp.max(
            jnp.where(owner[:, :, :, None] > 0, pair_top[:, :, None, :], NEGATIVE), axis=(0, 1)
        )
        col_top = lax.pmax(local_col_top, "row")
        chosen_top = jnp.take(col_top, neighbor_ids, axis=0)
        part = jnp.sum(
            jnp.where(live, jnp.exp(col_scores - chosen_top[:, :, None, :]), 0.0), axis=2
        )
        col_total = lax.psum(
            jnp.einsum("rkc,rkq->cq", owner, part, precision=lax.Precision.HIGHEST), "row"
        )
        true_pot = (EPSILON * (log_true - col_top - jnp.log(col_total))).reshape(-1)
    return (pred_pot.reshape(-1), true_pot)


def solution(mesh):
    in_specs = (P("row", None), P("col", None), P("row", "col", None), P("row", None))
    out_specs = (P("row"), P("col"))
    return jax.shard_map(
        on_device, mesh=mesh, in_specs=in_specs, out_specs=out_specs, check_vma=False
    )
```

profile of v0, /device:TPU:1, one launch (start us, length us, event | category | flops | bytes accessed | tf_op | source)
XLA Modules:
  0.0 1652.7 jit_solution(16729835161534090191)
XLA Ops:
  7.2 2.2 multiply_reduce_fusion
  9.4 2.2 copy_bitcast_fusion
  12.3 2.5 sort.17
  19.7 2.2 gather_fusion.5
  24.1 8.9 fusion.4
  33.8 61.7 %pmax.42 = f32[80,128]{1,0:T(8,128)S(1)} all-reduce(f32[80,128]{1,0:T(8,128)S(1)} %scatter_custom_fusion), channel_id=1, replica_groups=mesh['row'=32,'col'=16] {'col'}, use_global_device_ids=true, to_apply=%region_5.8 | all-reduce | flops 10240 | bytes 81920 | tf_op jit(solution)/shard_map/pmax | solution.py:61
  96.1 6.1 select_reduce_fusion.8
  103.0 55.9 %psum.42 = f32[80,128]{1,0:T(8,128)S(1)} all-reduce(f32[80,128]{1,0:T(8,128)S(1)} %scatter_custom_fusion.1), channel_id=1, replica_groups=mesh['row'=32,'col'=16] {'col'}, use_global_device_ids=true, to_apply=%region_8.12 | all-reduce | flops 10240 | bytes 81920 | tf_op jit(solution)/shard_map/psum | solution.py:66
  159.5 15.8 select_reduce_fusion.7
  176.1 210.7 %all-reduce.7.cloned.1.call-done = f32[128,128]{1,0:T(8,128)} async-done(((f32[128,128]{1,0:T(8,128)}), f32[128,128]{1,0:T(8,128)}) %all-reduce.7.cloned.1.call-update) | async-done | bytes 65552 | tf_op jit(solution)/shard_map/pmax | solution.py:77
  386.8 1.6 gather_fusion.8
  388.4 7.5 select_reduce_fusion.6
  397.2 176.4 %all-reduce.9.cloned.1.call-done = f32[128,128]{1,0:T(8,128)} async-done(((f32[128,128]{1,0:T(8,128)}), f32[128,128]{1,0:T(8,128)}) %all-reduce.9.cloned.1.call-update) | async-done | bytes 65552 | tf_op jit(solution)/shard_map/psum | solution.py:82
  575.2 5.8 fusion.5
  581.7 60.4 %pmax.44 = f32[80,128]{1,0:T(8,128)S(1)} all-reduce(f32[80,128]{1,0:T(8,128)S(1)} %scatter_custom_fusion.2), channel_id=1, replica_groups=mesh['row'=32,'col'=16] {'col'}, use_global_device_ids=true, to_apply=%region_16.20 | all-reduce | flops 10240 | bytes 81920 | tf_op jit(solution)/shard_map/pmax | solution.py:61
  642.8 6.1 select_reduce_fusion.5
  649.6 56.1 %psum.44 = f32[80,128]{1,0:T(8,128)S(1)} all-reduce(f32[80,128]{1,0:T(8,128)S(1)} %scatter_custom_fusion.3), channel_id=1, replica_groups=mesh['row'=32,'col'=16] {'col'}, use_global_device_ids=true, to_apply=%region_19.23 | all-reduce | flops 10240 | bytes 81920 | tf_op jit(solution)/shard_map/psum | solution.py:66
  706.4 15.8 select_reduce_fusion.4
  722.9 199.3 %all-reduce.11.cloned.1.call-done = f32[128,128]{1,0:T(8,128)} async-done(((f32[128,128]{1,0:T(8,128)}), f32[128,128]{1,0:T(8,128)}) %all-reduce.11.cloned.1.call-update) | async-done | bytes 65552 | tf_op jit(solution)/shard_map/pmax | solution.py:77
  922.2 1.6 gather_fusion.12
  923.9 7.5 select_reduce_fusion.3
  932.4 176.6 %all-reduce.13.cloned.1.call-done = f32[128,128]{1,0:T(8,128)} async-done(((f32[128,128]{1,0:T(8,128)}), f32[128,128]{1,0:T(8,128)}) %all-reduce.13.cloned.1.call-update) | async-done | bytes 65552 | tf_op jit(solution)/shard_map/psum | solution.py:82
  1110.6 5.8 fusion.6
  1117.1 60.4 %pmax.46 = f32[80,128]{1,0:T(8,128)S(1)} all-reduce(f32[80,128]{1,0:T(8,128)S(1)} %scatter_custom_fusion.4), channel_id=1, replica_groups=mesh['row'=32,'col'=16] {'col'}, use_global_device_ids=true, to_apply=%region_27.31 | all-reduce | flops 10240 | bytes 81920 | tf_op jit(solution)/shard_map/pmax | solution.py:61
  1178.2 6.1 select_reduce_fusion.2
  1185.0 55.9 %psum.46 = f32[80,128]{1,0:T(8,128)S(1)} all-reduce(f32[80,128]{1,0:T(8,128)S(1)} %scatter_custom_fusion.5), channel_id=1, replica_groups=mesh['row'=32,'col'=16] {'col'}, use_global_device_ids=true, to_apply=%region_30.34 | all-reduce | flops 10240 | bytes 81920 | tf_op jit(solution)/shard_map/psum | solution.py:66
  1241.6 15.8 select_reduce_fusion.1
  1258.2 199.4 %all-reduce.15.cloned.1.call-done = f32[128,128]{1,0:T(8,128)} async-done(((f32[128,128]{1,0:T(8,128)}), f32[128,128]{1,0:T(8,128)}) %all-reduce.15.cloned.1.call-update) | async-done | bytes 65552 | tf_op jit(solution)/shard_map/pmax | solution.py:77
  1457.6 1.6 gather_fusion.16
  1459.3 7.5 select_reduce_fusion
  1467.8 176.6 %all-reduce.17.cloned.1.call-done = f32[128,128]{1,0:T(8,128)} async-done(((f32[128,128]{1,0:T(8,128)}), f32[128,128]{1,0:T(8,128)}) %all-reduce.17.cloned.1.call-update) | async-done | bytes 65552 | tf_op jit(solution)/shard_map/psum | solution.py:82
  1644.4 1.5 multiply_bitcast_fusion
  (95 shorter events, 25.1 us)
Async XLA Ops:
  7.2 14.7 copy-start
  7.2 379.6 %all-reduce.7.cloned.1.call-start = ((), (), s32[]{:S(2)}) async-start(), calls=%async_computation | async-start | bytes 131072 | tf_op jit(solution)/shard_map/pmax | solution.py:77
  14.9 1.5 copy-start.9
  14.9 2.2 copy-start.5
  14.9 2.2 copy-start.7
  19.0 3.2 copy-start.8
  19.1 3.8 copy-start.6
  176.0 397.6 %all-reduce.9.cloned.1.call-start = ((), (), s32[]{:S(2)}) async-start(), calls=%async_computation.1 | async-start | bytes 131072 | tf_op jit(solution)/shard_map/psum | solution.py:82
  386.8 186.8 %copy-start.2 = (f32[128,128]{1,0:T(8,128)S(1)}, f32[128,128]{1,0:T(8,128)}, u32[]{:S(2)}) copy-start(f32[128,128]{1,0:T(8,128)} %all-reduce.7.cloned.1.call-done) | copy-start | bytes 196612
  396.9 525.3 %all-reduce.11.cloned.1.call-start = ((), (), s32[]{:S(2)}) async-start(), calls=%async_computation.2 | async-start | bytes 131072 | tf_op jit(solution)/shard_map/pmax | solution.py:77
  722.9 386.1 %all-reduce.13.cloned.1.call-start = ((), (), s32[]{:S(2)}) async-start(), calls=%async_computation.3 | async-start | bytes 131072 | tf_op jit(solution)/shard_map/psum | solution.py:82
  922.2 186.8 %copy-start.3 = (f32[128,128]{1,0:T(8,128)S(1)}, f32[128,128]{1,0:T(8,128)}, u32[]{:S(2)}) copy-start(f32[128,128]{1,0:T(8,128)} %all-reduce.11.cloned.1.call-done) | copy-start | bytes 196612
  932.4 525.2 %all-reduce.15.cloned.1.call-start = ((), (), s32[]{:S(2)}) async-start(), calls=%async_computation.4 | async-start | bytes 131072 | tf_op jit(solution)/shard_map/pmax | solution.py:77
  1241.0 225.7 %copy-start.4 = (f32[80,128]{1,0:T(8,128)}, f32[80,128]{1,0:T(8,128)S(1)}, u32[]{:S(2)}) copy-start(f32[80,128]{1,0:T(8,128)S(1)} %compare_select_fusion) | copy-start | bytes 122884
  1258.2 386.2 %all-reduce.17.cloned.1.call-start = ((), (), s32[]{:S(2)}) async-start(), calls=%async_computation.5 | async-start | bytes 131072 | tf_op jit(solution)/shard_map/psum | solution.py:82
  1457.6 186.8 %copy-start.1 = (f32[128,128]{1,0:T(8,128)S(1)}, f32[128,128]{1,0:T(8,128)}, u32[]{:S(2)}) copy-start(f32[128,128]{1,0:T(8,128)} %all-reduce.15.cloned.1.call-done) | copy-start | bytes 196612
Sparse Core Ops, SparseCore 0:
  176.1 210.6 all-reduce.6
  397.1 176.4 all-reduce.8
  723.0 199.1 all-reduce.10
  932.5 176.4 all-reduce.12
  1258.3 199.2 all-reduce.14
  1467.9 176.4 all-reduce.16
where the time goes:
time: 1650 us
  waiting for transfers between devices  1140 us (69%)
  blocking collectives  350 us (21%)
  other arithmetic  111 us (7%)
  local copies, waits for them, and re-layouts  25.8 us (2%)
    pmax x3, waiting for transfers between devices, on_device(): col_top = lax.pmax(local_col_top, 'row')  609 us
    psum x3, waiting for transfers between devices, on_device(): lax.psum(jnp.einsum('rkc,rkq->cq', owner, part, precision=lax.Precision.H...  530 us
    pmax x3, blocking collectives, on_device(): top = lax.pmax(spread(local_top, NEGATIVE), 'col')  182 us
    psum x3, blocking collectives, on_device(): total = lax.psum(spread(local_total, 0.0), 'col')  168 us
    broadcast_in_dim x3, other arithmetic, on_device(): jnp.where(owner[:, :, :, None] > 0, pair_top[:, :, None, :], NEGATIVE)  47.3 us
  transfers between devices with their start and end apart: 6, of which 6 were waited for; matrix products, arithmetic and copies ran while one was open for 0% of the time, Pallas kernels for 0%

commit v1 on v0

v1 whole, which is shorter than its diff:
```python
import functools
import math

import jax
import jax.numpy as jnp
from jax import lax
from jax.experimental import pallas as pl
from jax.experimental.pallas import tpu as pltpu
from jax.sharding import PartitionSpec as P

BLOCK = 128
ITERS = 3
EPSILON = 0.02
NEGATIVE = -1e30
TILE = 8
CORES = 2
LISTS = 16
PICK_LANE = 63
UNIT = 1.0 / (EPSILON * math.log(2.0))
MESH = pl.DeviceIdType.MESH
F32, BF16, I32 = jnp.float32, jnp.bfloat16, jnp.int32


def dot(a, b, b_axis):
    return lax.dot_general(a, b, (((1,), (b_axis,)), ((), ())), preferred_element_type=F32)


def iota(shape, axis):
    return lax.broadcasted_iota(I32, shape, axis)


def join(a, b):
    high, low = jnp.maximum(a, b), jnp.minimum(a, b)
    return high + jnp.log2(1.0 + jnp.exp2(low - high))


def tree(op, items):
    items = list(items)
    while len(items) > 1:
        items = [op(*items[i : i + 2]) if i + 1 < len(items) else items[i] for i in range(0, len(items), 2)]
    return items[0]


def top_and_total(items):
    top = tree(jnp.maximum, items)
    return top, tree(jnp.add, [jnp.exp2(item - top) for item in items])


def square_norms(block):
    wide = block.astype(F32)
    return jnp.sum(wide * wide, axis=0, keepdims=True)


def block_of(features, index):
    return features[:, pl.ds(pl.multiple_of(BLOCK * index, BLOCK), BLOCK)]


def slot_row(b, homes):
    return jnp.where(b < homes, b, b + (TILE - homes))


def prepare_kernel(
    ncol, homes, counts_ref, neighbors_ref, pred_hbm, true_hbm, table_ref, onehot, cost, pred_norm, true_norm,
    pred, true, table, load_sem,
):
    here = lax.axis_index("col")
    width, cblocks = true.shape[0], true_norm.shape[0]
    slots = 2 * homes
    loads = [
        pltpu.make_async_copy(true_hbm, true, load_sem.at[0]),
        pltpu.make_async_copy(pred_hbm, pred, load_sem.at[1]),
    ]
    for load in loads:
        load.start()
    counts = counts_ref[...].astype(F32)
    blocks, kmax = counts.shape[1], neighbors_ref.shape[0]
    to, frm = iota((ncol, ncol), 0), iota((ncol, ncol), 1)
    before = (frm == lax.rem(to + (ncol - 1), ncol)).astype(F32)
    home = ((counts > 0.5) & (dot(before, counts, 0) < 0.5)).astype(F32)
    upto = (iota((blocks, blocks), 0) <= iota((blocks, blocks), 1)).astype(F32)
    rank = dot(home, upto, 0) - 1.0
    shard = iota(home.shape, 0).astype(F32)
    place = jnp.sum(home * (TILE * shard + rank), axis=0, keepdims=True)
    slot = iota((2 * TILE, blocks), 0)
    owner = jnp.where(slot < TILE, here, lax.rem(here + (ncol - 1), ncol))
    wanted = (TILE * owner + lax.rem(slot, TILE)).astype(F32)
    chosen = (place == wanted).astype(F32)
    count = jnp.sum(jnp.where(iota(counts.shape, 0) == here, counts, 0.0), axis=0, keepdims=True)
    count = jnp.sum(chosen * count, axis=1, keepdims=True)
    pick = jnp.sum(chosen * iota(chosen.shape, 1).astype(F32), axis=1, keepdims=True)
    lane = iota((kmax, BLOCK), 1)
    repeat = ((lax.rem(lane, LISTS) == iota((kmax, BLOCK), 0)) & (lane < 3 * LISTS)).astype(F32)
    listed = dot(dot(chosen, neighbors_ref[:, 0, :].astype(F32), 1), repeat, 0)
    lane = iota(listed.shape, 1)
    live = lax.rem(lane, LISTS).astype(F32) < count
    found = jnp.where(lane == PICK_LANE, pick, jnp.where(live, listed, float(cblocks)))
    table_ref[0 : 2 * TILE, :] = found.astype(I32)
    table_ref[2 * TILE : 3 * TILE, :] = jnp.zeros((TILE, BLOCK), I32)
    table_ref[2 * TILE : 2 * TILE + 1, 0:blocks] = place.astype(I32)
    to_scalar = pltpu.make_async_copy(table_ref, table, load_sem.at[2])
    to_scalar.start()

    def match_blocks(b, carry):
        listed = table_ref[pl.ds(slot_row(b, homes), 1), 0 : 4 * LISTS]
        lane = iota((cblocks, 4 * LISTS), 1)
        match = ((iota((cblocks, 4 * LISTS), 0) == listed) & (lane < 3 * LISTS)).astype(F32)
        absent = 1.0 - jnp.sum(jnp.where(lane < LISTS, match, 0.0), axis=1, keepdims=True)
        onehot[b] = jnp.where(lane == 3 * LISTS, absent, match).astype(BF16)
        return carry

    lax.fori_loop(0, slots, match_blocks, 0)

    loads[0].wait()

    def norm_row(i, carry):
        true_norm[pl.ds(i, 1), :] = square_norms(block_of(true, i)) * (UNIT / width)
        return carry

    lax.fori_loop(0, cblocks, norm_row, 0, unroll=8)
    loads[1].wait()
    to_scalar.wait()
    pred_norm[...] = jnp.zeros((TILE, BLOCK), F32)
    for b in range(homes):
        pred_norm[b : b + 1, :] = square_norms(block_of(pred, table[b, PICK_LANE])) * (UNIT / width)

    def products(b, carry):
        at = slot_row(b, homes)
        mine = jnp.transpose(block_of(pred, table[at, PICK_LANE]))
        for k in range(neighbors_ref.shape[0]):
            other = block_of(true, jnp.minimum(table[at, k], cblocks - 1))
            cost[b * kmax + k] = dot(mine, other, 0) * (2.0 * UNIT / width)
        return carry

    lax.fori_loop(0, slots, products, 0)


def sinkhorn_kernel(
    sizes, table, onehot, cost, pred_norm, true_norm, pred_out, true_out,
    potential, columns, tops, sums, spread,
    part, parts, mate_out, mate_in, share, swap_out, swap_in, last_out, last_in,
    part_send, part_recv, mate_send, mate_recv, share_send, share_recv, swap_send, swap_recv,
    last_send, last_recv,
):
    nz, ncol, homes, kmax, log_a, log_b = sizes
    row, col = lax.axis_index("row"), lax.axis_index("col")
    z, core = row // CORES, lax.rem(row, CORES)
    slots = 2 * homes
    cblocks = true_norm.shape[0]
    right, left = lax.rem(col + 1, ncol), lax.rem(col + (ncol - 1), ncol)

    def far_first(i, n):
        return n // 2 + (1 - 2 * lax.rem(i, 2)) * ((i + 1) // 2)

    def along_z(d):
        return {"row": lax.rem(z + d, nz) * CORES + core}

    barrier = pltpu.get_barrier_semaphore()

    def greet_z(i, carry):
        pl.semaphore_signal(barrier, inc=1, device_id=along_z(i), device_id_type=MESH)
        return carry

    def greet_col(i, carry):
        pl.semaphore_signal(barrier, inc=1, device_id={"col": lax.rem(col + i, ncol)}, device_id_type=MESH)
        return carry

    lax.fori_loop(1, nz, greet_z, 0)
    lax.fori_loop(1, ncol, greet_col, 0)
    pl.semaphore_signal(barrier, inc=1, device_id={"row": z * CORES + (1 - core)}, device_id_type=MESH)

    for step in range(ITERS):
        potential[step, cblocks : cblocks + TILE, :] = jnp.full((TILE, BLOCK), NEGATIVE, F32)
    columns[...] = jnp.zeros((BLOCK, BLOCK), F32)

    def fill(b, carry):
        tops[b] = jnp.zeros((LISTS, BLOCK), F32)
        sums[b] = jnp.ones((LISTS, BLOCK), F32)
        return carry

    lax.fori_loop(0, slots, fill, 0)

    def share_copy(stage, d):
        return pltpu.make_async_remote_copy(
            src_ref=share.at[stage],
            dst_ref=potential.at[stage, pl.ds(TILE * z, TILE)],
            send_sem=share_send.at[stage, d],
            recv_sem=share_recv.at[stage, d],
            device_id=along_z(d),
            device_id_type=MESH,
        )

    def share_start(stage, value):
        share[stage] = value
        potential[stage, pl.ds(pl.multiple_of(TILE * z, TILE), TILE), :] = value

        def send(i, carry):
            share_copy(stage, far_first(i, nz)).start()
            return carry

        lax.fori_loop(0, nz - 1, send, 0)

    def share_wait(stage):
        def wait(i, carry):
            d = far_first(nz - 2 - i, nz)
            frm = lax.rem(z + (nz - d), nz)
            pltpu.make_async_remote_copy(
                src_ref=share.at[stage],
                dst_ref=potential.at[stage, pl.ds(TILE * frm, TILE)],
                send_sem=share_send.at[stage, d],
                recv_sem=share_recv.at[stage, d],
                device_id=along_z(d),
                device_id_type=MESH,
            ).wait()
            return carry

        lax.fori_loop(0, nz - 1, wait, 0)

    def block_of(features, index):
        return features[:, pl.ds(pl.multiple_of(BLOCK * index, BLOCK), BLOCK)]

    potential[0, 0:cblocks, :] = -true_norm[...]
    pl.semaphore_wait(barrier, nz + ncol - 1)

    def iteration(step, carry):
        def over_true(b, carry):
            at = slot_row(b, homes)
            near = [potential[step, pl.ds(table[at, k], 1), :] for k in range(kmax)]

            def rows(i, carry):
                here = pl.ds(pl.multiple_of(2 * TILE * i, 2 * TILE), 2 * TILE)
                top, total = top_and_total([cost[b * kmax + k, here, :] + near[k] for k in range(kmax)])
                high = jnp.max(top, axis=1, keepdims=True)
                total = jnp.sum(total * jnp.exp2(top - high), axis=1, keepdims=True)
                columns[here, :] = jnp.where(iota((2 * TILE, BLOCK), 1) == at, high + jnp.log2(total), columns[here, :])
                return carry

            lax.fori_loop(0, BLOCK // (2 * TILE), rows, 0, unroll=2)
            return carry

        lax.fori_loop(0, slots, over_true, 0)
        swap_out[step] = jnp.transpose(columns[...])[0 : 2 * TILE, :]

        def swap_copy(near):
            return pltpu.make_async_remote_copy(
                src_ref=swap_out.at[step, pl.ds(0 if near else TILE, TILE)],
                dst_ref=swap_in.at[step, pl.ds(TILE if near else 0, TILE)],
                send_sem=swap_send.at[step, int(near)],
                recv_sem=swap_recv.at[step, int(near)],
                device_id={"col": right if near else left},
                device_id_type=MESH,
            )

        for near in (True, False):
            swap_copy(near).start()
        for near in (True, False):
            swap_copy(near).wait()
        pred_rows = log_a - join(swap_out[step], swap_in[step])

        def last_copy(d, frm):
            return pltpu.make_async_remote_copy(
                src_ref=last_out,
                dst_ref=last_in.at[pl.ds(TILE * frm, TILE)],
                send_sem=last_send.at[d],
                recv_sem=last_recv.at[d],
                device_id={"col": lax.rem(col + d, ncol)},
                device_id_type=MESH,
            )

        @pl.when(step == ITERS - 1)
        def _():
            final = (pred_rows[0:TILE, :] + pred_norm[...]) * (1.0 / UNIT)
            last_out[...] = final
            last_in[pl.ds(pl.multiple_of(TILE * col, TILE), TILE), :] = final

            def send(i, carry):
                last_copy(far_first(i, ncol), col).start()
                return carry

            lax.fori_loop(0, ncol - 1, send, 0)

        columns[...] = jnp.transpose(jnp.concatenate([pred_rows, jnp.zeros((BLOCK - 2 * TILE, BLOCK), F32)], axis=0))

        def over_pred(b, carry):
            at = slot_row(b, homes)
            mine = []
            for i in range(BLOCK // TILE):
                held = columns[i * TILE : (i + 1) * TILE, :]
                picked = jnp.sum(jnp.where(iota((TILE, BLOCK), 1) == at, held, 0.0), axis=1, keepdims=True)
                mine.append(jnp.broadcast_to(picked, (TILE, BLOCK)))
            for k in range(kmax):
                top, total = top_and_total(
                    [cost[b * kmax + k, i * TILE : (i + 1) * TILE, :] + mine[i] for i in range(BLOCK // TILE)]
                )
                high = jnp.max(top, axis=0, keepdims=True)
                tops[b, k : k + 1, :] = high
                sums[b, k : k + 1, :] = jnp.sum(total * jnp.exp2(top - high), axis=0, keepdims=True)
            return carry

        lax.fori_loop(0, slots, over_pred, 0)

        def expand(b, carry):
            value = tops[b] + jnp.log2(sums[b])
            first = value.astype(BF16)
            rest = value - first.astype(F32)
            second = rest.astype(BF16)
            third = (rest - second.astype(F32)).astype(BF16)
            none = jnp.where(iota((LISTS, BLOCK), 0) == 0, NEGATIVE, 0.0).astype(BF16)
            spread[b] = dot(onehot[b], jnp.concatenate([first, second, third, none], axis=0), 0)
            return carry

        lax.fori_loop(0, slots, expand, 0)

        def gather(i, carry):
            here = pl.ds(pl.multiple_of(TILE * i, TILE), TILE)
            top, total = top_and_total([spread[b, here, :] for b in range(slots)])
            part[step, here, :] = top + jnp.log2(total)
            return carry

        lax.fori_loop(0, cblocks // TILE, gather, 0, unroll=2)

        def part_copy(d, to, frm):
            return pltpu.make_async_remote_copy(
                src_ref=part.at[step, pl.ds(TILE * to, TILE)],
                dst_ref=parts.at[step, pl.ds(TILE * frm, TILE)],
                send_sem=part_send.at[step, d],
                recv_sem=part_recv.at[step, d],
                device_id=along_z(d),
                device_id_type=MESH,
            )

        def part_start(i, carry):
            d = far_first(i, nz)
            part_copy(d, lax.rem(z + d, nz), z).start()
            return carry

        def part_wait(i, carry):
            d = far_first(nz - 2 - i, nz)
            part_copy(d, lax.rem(z + d, nz), lax.rem(z + (nz - d), nz)).wait()
            return carry

        lax.fori_loop(0, nz - 1, part_start, 0)
        own = pl.ds(pl.multiple_of(TILE * z, TILE), TILE)
        parts[step, own, :] = part[step, own, :]
        lax.fori_loop(0, nz - 1, part_wait, 0)
        top, total = top_and_total([parts[step, i * TILE : (i + 1) * TILE, :] for i in range(nz)])
        mate_out[step] = top + jnp.log2(total)
        mate = pltpu.make_async_remote_copy(
            src_ref=mate_out.at[step],
            dst_ref=mate_in.at[step],
            send_sem=mate_send.at[step],
            recv_sem=mate_recv.at[step],
            device_id={"row": z * CORES + (1 - core)},
            device_id_type=MESH,
        )
        mate.start()
        mate.wait()
        fresh = log_b - join(mate_out[step], mate_in[step])
        share_start(step + 1, jnp.where(step == ITERS - 1, (fresh + true_norm[own, :]) * (1.0 / UNIT), fresh))

        @pl.when(step == ITERS - 1)
        def _():
            def wait(i, carry):
                d = far_first(ncol - 2 - i, ncol)
                last_copy(d, lax.rem(col + (ncol - d), ncol)).wait()
                return carry

            lax.fori_loop(0, ncol - 1, wait, 0)

            def place(i, carry):
                pred_out[pl.ds(i, 1), :] = last_in[pl.ds(table[2 * TILE, i], 1), :]
                return carry

            lax.fori_loop(0, pred_out.shape[0], place, 0, unroll=8)

        share_wait(step + 1)
        return carry

    lax.fori_loop(0, ITERS, iteration, 0)
    true_out[...] = potential[ITERS, 0:cblocks, :]


def on_device(pred_feat, true_feat, neighbors, counts):
    width = pred_feat.shape[1]
    rblocks, cblocks = pred_feat.shape[0] // BLOCK, true_feat.shape[0] // BLOCK
    nrow, ncol = lax.axis_size("row"), lax.axis_size("col")
    nz, homes, kmax = nrow // CORES, rblocks // ncol, neighbors.shape[2]
    slots = 2 * homes
    log_a = -math.log2(pred_feat.shape[0] * nrow)
    log_b = -math.log2(true_feat.shape[0] * ncol)
    vmem = pl.BlockSpec(memory_space=pltpu.VMEM)
    anywhere = pl.BlockSpec(memory_space=pl.ANY)
    dma = pltpu.SemaphoreType.DMA
    ready = pl.pallas_call(
        functools.partial(prepare_kernel, ncol, homes),
        out_shape=(
            jax.ShapeDtypeStruct((3 * TILE, BLOCK), I32),
            jax.ShapeDtypeStruct((slots, cblocks, 4 * LISTS), BF16),
            jax.ShapeDtypeStruct((slots * kmax, BLOCK, BLOCK), F32),
            jax.ShapeDtypeStruct((TILE, BLOCK), F32),
            jax.ShapeDtypeStruct((cblocks, BLOCK), F32),
        ),
        in_specs=[vmem, vmem, anywhere, anywhere],
        out_specs=(vmem,) * 5,
        scratch_shapes=[
            pltpu.VMEM((width, rblocks * BLOCK), BF16),
            pltpu.VMEM((width, cblocks * BLOCK), BF16),
            pltpu.SMEM((3 * TILE, BLOCK), I32),
            dma((3,)),
        ],
        compiler_params=pltpu.CompilerParams(vmem_limit_bytes=24 * 2**20),
        name="prepare",
    )(counts.T, jnp.transpose(neighbors, (2, 1, 0)), pred_feat.T, true_feat.T)
    pred_pot, true_pot = pl.pallas_call(
        functools.partial(sinkhorn_kernel, (nz, ncol, homes, kmax, log_a, log_b)),
        out_shape=(
            jax.ShapeDtypeStruct((rblocks, BLOCK), F32),
            jax.ShapeDtypeStruct((cblocks, BLOCK), F32),
        ),
        in_specs=[
            pl.BlockSpec(memory_space=pltpu.SMEM),
            vmem,
            vmem,
            vmem,
            vmem,
        ],
        out_specs=(vmem, vmem),
        scratch_shapes=[
            pltpu.VMEM((ITERS + 1, cblocks + TILE, BLOCK), F32),
            pltpu.VMEM((BLOCK, BLOCK), F32),
            pltpu.VMEM((slots, LISTS, BLOCK), F32),
            pltpu.VMEM((slots, LISTS, BLOCK), F32),
            pltpu.VMEM((slots, cblocks, BLOCK), F32),
            pltpu.VMEM((ITERS, cblocks, BLOCK), F32),
            pltpu.VMEM((ITERS, cblocks, BLOCK), F32),
            pltpu.VMEM((ITERS, TILE, BLOCK), F32),
            pltpu.VMEM((ITERS, TILE, BLOCK), F32),
            pltpu.VMEM((ITERS + 1, TILE, BLOCK), F32),
            pltpu.VMEM((ITERS, 2 * TILE, BLOCK), F32),
            pltpu.VMEM((ITERS, 2 * TILE, BLOCK), F32),
            pltpu.VMEM((TILE, BLOCK), F32),
            pltpu.VMEM((TILE * ncol, BLOCK), F32),
            dma((ITERS, nz)),
            dma((ITERS, nz)),
            dma((ITERS,)),
            dma((ITERS,)),
            dma((ITERS + 1, nz)),
            dma((ITERS + 1, nz)),
            dma((ITERS, 2)),
            dma((ITERS, 2)),
            dma((ncol,)),
            dma((ncol,)),
        ],
        compiler_params=pltpu.CompilerParams(
            collective_id=0, has_side_effects=True, vmem_limit_bytes=24 * 2**20
        ),
        name="sinkhorn",
    )(*ready)
    return (pred_pot.reshape(-1), true_pot.reshape(-1))


def solution(mesh):
    in_specs = (P("row", None), P("col", None), P("row", "col", None), P("row", None))
    out_specs = (P("row"), P("col"))
    return jax.shard_map(
        on_device, mesh=mesh, in_specs=in_specs, out_specs=out_specs, check_vma=False
    )
```

time: 1650 us -> 129 us (0.08)
  waiting for transfers between devices: 1140 us -> 0 us
  blocking collectives: 350 us -> 0 us
  Pallas kernels: 0 us -> 123 us
  other arithmetic: 111 us -> 0 us
  local copies, waits for them, and re-layouts: 25.8 us -> 5.54 us
    pmax x3 -> x0, waiting for transfers between devices: 609 us -> none  [on_device(): col_top = lax.pmax(local_col_top, 'row')]
    psum x3 -> x0, waiting for transfers between devices: 530 us -> none  [on_device(): lax.psum(jnp.einsum('rkc,rkq->cq', owner, part, precision=lax.Precision.H...]
    pmax x3 -> x0, blocking collectives: 182 us -> none  [on_device(): top = lax.pmax(spread(local_top, NEGATIVE), 'col')]
    psum x3 -> x0, blocking collectives: 168 us -> none  [on_device(): total = lax.psum(spread(local_total, 0.0), 'col')]
    pallas_call x0 -> x2, Pallas kernels: none -> 123 us  [the longest x1 117 us: on_device(): pl.pallas_call(functools.partial(sinkhorn_kernel, (nz, ncol, homes, kmax,...]
    broadcast_in_dim x3 -> x0, other arithmetic: 47.3 us -> none  [on_device(): jnp.where(owner[:, :, :, None] > 0, pair_top[:, :, None, :], NEGATIVE)]
    reduce_sum x8 -> x0, other arithmetic: 43.1 us -> none  [the longest x3 22.4 us: on_device(): jnp.sum(jnp.where(live, jnp.exp(col_scores - chosen_top[:, :, None, :]),...]
  transfers between devices with their start and end apart: 6 -> 0, of which waited for: 6 -> 0; matrix products, arithmetic and copies ran while one was open for 0% -> 0% of each run, Pallas kernels for 0% -> 0%
where the time goes in v1:
time: 129 us
  Pallas kernels  123 us (95%)
  local copies, waits for them, and re-layouts  5.54 us (4%)
    pallas_call x1, Pallas kernels, on_device(): pl.pallas_call(functools.partial(sinkhorn_kernel, (nz, ncol, homes, kmax,...  117 us
    unnamed x10, local copies, waits for them, and re-layouts  5.54 us
    pallas_call x1, Pallas kernels, on_device(): pl.pallas_call(functools.partial(prepare_kernel, ncol, homes), out_shape=...  5.48 us

profile of v1, /device:TPU:1, one launch (start us, length us, event | category | flops | bytes accessed | tf_op | source)
XLA Modules:
  0.0 129.1 jit_solution(1667309673893678356)
XLA Ops:
  0.6 0.0 copy-start
  0.6 1.6 %copy-done = bf16[16384,64]{0,1:T(8,128)(2,1)S(1)} copy-done((bf16[16384,64]{0,1:T(8,128)(2,1)S(1)}, bf16[16384,64]{0,1:T(8,128)(2,1)}, u32[]{:S(2)}) %copy-start) | copy-done | bytes 2097176
  2.2 0.0 copy-start.1
  2.2 1.3 %copy-done.1 = bf16[10240,64]{0,1:T(8,128)(2,1)S(1)} copy-done((bf16[10240,64]{0,1:T(8,128)(2,1)S(1)}, bf16[10240,64]{0,1:T(8,128)(2,1)}, u32[]{:S(2)}) %copy-start.1) | copy-done | bytes 1310744
  3.5 0.0 copy-start.2
  3.5 0.7 copy-done.2
  4.2 0.0 copy-start.3
  4.2 0.7 copy-done.3
  4.9 5.5 %prepare.1 = (s32[24,128]{1,0:T(8,128)S(1)}, bf16[10,128,64]{2,1,0:T(8,128)(2,1)S(1)}, f32[120,128,128]{2,1,0:T(8,128)S(1)}, f32[8,128]{1,0:T(8,128)S(1)}, f32[128,128]{1,0:T(8,128)S(1)}) custom-call(s32[16,80]{1,0:T(8,128)S(1)} %bitcast.10, s32[12,1,80]{2,1,0:T(1,128)S(1)} %bitcast.11, bf16[64,10240]{1,0:T(8,128)(2,1)S(1)} %bitcast.7, ...), custom_call_target="tpu_custom_call" | custom-call | tf_op jit(solution)/shard_map/prepare/pallas_call | solution.py:393
  10.4 117.4 %sinkhorn.1 = (f32[80,128]{1,0:T(8,128)S(1)}, f32[128,128]{1,0:T(8,128)S(1)}) custom-call(s32[24,128]{1,0:T(8,128)S(1)} %get-tuple-element.9.table, bf16[10,128,64]{2,1,0:T(8,128)(2,1)S(1)} %get-tuple-element.10.onehot, f32[120,128,128]{2,1,0:T(8,128)S(1)} %get-tuple-element.11.cost, f32[8,128]{1,0:T(8,128)S(1)} %get-tuple-element.12.pred_norm, ...), custom_call_target="tpu_custom_call" | custom-call | tf_op jit(solution)/shard_map/sinkhorn/pallas_call | solution.py:413
  127.8 0.6 copy.8
  128.5 0.6 copy.9
Async XLA Ops:
  0.6 1.6 %copy-start = (bf16[16384,64]{0,1:T(8,128)(2,1)S(1)}, bf16[16384,64]{0,1:T(8,128)(2,1)}, u32[]{:S(2)}) copy-start(bf16[16384,64]{0,1:T(8,128)(2,1)} %param.5) | copy-start | bytes 6291460
  2.2 1.3 %copy-start.1 = (bf16[10240,64]{0,1:T(8,128)(2,1)S(1)}, bf16[10240,64]{0,1:T(8,128)(2,1)}, u32[]{:S(2)}) copy-start(bf16[10240,64]{0,1:T(8,128)(2,1)} %param.4) | copy-start | bytes 3932164
  3.5 0.7 copy-start.2
  4.2 0.7 copy-start.3

commit v2 on v1

v2 whole, which is shorter than its diff:
```python
import functools
import math

import jax
import jax.numpy as jnp
from jax import lax
from jax.experimental import pallas as pl
from jax.experimental.pallas import tpu as pltpu
from jax.sharding import PartitionSpec as P

BLOCK = 128
ITERS = 3
EPSILON = 0.02
NEGATIVE = -1e30
TILE = 8
CORES = 2
ROWS = 16
OWNERS = 4
LISTS = 16
PICK_LANE = 63
UNIT = 1.0 / (EPSILON * math.log(2.0))
MESH = pl.DeviceIdType.MESH
F32, BF16, I32 = jnp.float32, jnp.bfloat16, jnp.int32


def dot(a, b, b_axis):
    return lax.dot_general(a, b, (((1,), (b_axis,)), ((), ())), preferred_element_type=F32)


def iota(shape, axis):
    return lax.broadcasted_iota(I32, shape, axis)


def join(a, b):
    high, low = jnp.maximum(a, b), jnp.minimum(a, b)
    return high + jnp.log2(1.0 + jnp.exp2(low - high))


def tree(op, items):
    items = list(items)
    while len(items) > 1:
        items = [op(*items[i : i + 2]) if i + 1 < len(items) else items[i] for i in range(0, len(items), 2)]
    return items[0]


def top_and_total(items):
    top = tree(jnp.maximum, items)
    return top, tree(jnp.add, [jnp.exp2(item - top) for item in items])


def square_norms(block):
    wide = block.astype(F32)
    return jnp.sum(wide * wide, axis=0, keepdims=True)


def block_of(features, index):
    return features[:, pl.ds(pl.multiple_of(BLOCK * index, BLOCK), BLOCK)]


def slot_row(b, homes):
    return jnp.where(b < homes, b, b + (TILE - homes))


def prepare_kernel(
    ncol, homes, counts_ref, neighbors_ref, pred_hbm, true_hbm, table_ref, onehot, cost, pred_norm, true_norm,
    pred, true, table, load_sem,
):
    here = lax.axis_index("col")
    width, cblocks = true.shape[0], true_norm.shape[0]
    slots = 2 * homes
    loads = [
        pltpu.make_async_copy(true_hbm, true, load_sem.at[0]),
        pltpu.make_async_copy(pred_hbm, pred, load_sem.at[1]),
    ]
    for load in loads:
        load.start()
    counts = counts_ref[...].astype(F32)
    blocks, kmax = counts.shape[1], neighbors_ref.shape[0]
    to, frm = iota((ncol, ncol), 0), iota((ncol, ncol), 1)
    before = (frm == lax.rem(to + (ncol - 1), ncol)).astype(F32)
    home = ((counts > 0.5) & (dot(before, counts, 0) < 0.5)).astype(F32)
    upto = (iota((blocks, blocks), 0) <= iota((blocks, blocks), 1)).astype(F32)
    rank = dot(home, upto, 0) - 1.0
    shard = iota(home.shape, 0).astype(F32)
    place = jnp.sum(home * (TILE * shard + rank), axis=0, keepdims=True)
    slot = iota((2 * TILE, blocks), 0)
    owner = jnp.where(slot < TILE, here, lax.rem(here + (ncol - 1), ncol))
    wanted = (TILE * owner + lax.rem(slot, TILE)).astype(F32)
    chosen = (place == wanted).astype(F32)
    count = jnp.sum(jnp.where(iota(counts.shape, 0) == here, counts, 0.0), axis=0, keepdims=True)
    count = jnp.sum(chosen * count, axis=1, keepdims=True)
    pick = jnp.sum(chosen * iota(chosen.shape, 1).astype(F32), axis=1, keepdims=True)
    lane = iota((kmax, BLOCK), 1)
    repeat = ((lax.rem(lane, LISTS) == iota((kmax, BLOCK), 0)) & (lane < 3 * LISTS)).astype(F32)
    listed = dot(dot(chosen, neighbors_ref[:, 0, :].astype(F32), 1), repeat, 0)
    lane = iota(listed.shape, 1)
    live = lax.rem(lane, LISTS).astype(F32) < count
    found = jnp.where(lane == PICK_LANE, pick, jnp.where(live, listed, float(cblocks)))
    table_ref[0 : 2 * TILE, :] = found.astype(I32)
    table_ref[2 * TILE : 3 * TILE, :] = jnp.zeros((TILE, BLOCK), I32)
    table_ref[2 * TILE : 2 * TILE + 1, 0:blocks] = place.astype(I32)
    to_scalar = pltpu.make_async_copy(table_ref, table, load_sem.at[2])
    to_scalar.start()

    def match_blocks(b, carry):
        listed = table_ref[pl.ds(slot_row(b, homes), 1), 0 : 4 * LISTS]
        lane = iota((cblocks, 4 * LISTS), 1)
        match = ((iota((cblocks, 4 * LISTS), 0) == listed) & (lane < 3 * LISTS)).astype(F32)
        absent = 1.0 - jnp.sum(jnp.where(lane < LISTS, match, 0.0), axis=1, keepdims=True)
        onehot[b] = jnp.where(lane == 3 * LISTS, absent, match).astype(BF16)
        return carry

    lax.fori_loop(0, slots, match_blocks, 0)

    loads[0].wait()

    def norm_row(i, carry):
        true_norm[pl.ds(i, 1), :] = square_norms(block_of(true, i)) * (UNIT / width)
        return carry

    lax.fori_loop(0, cblocks, norm_row, 0, unroll=8)
    loads[1].wait()
    to_scalar.wait()
    pred_norm[...] = jnp.zeros((TILE, BLOCK), F32)
    for b in range(homes):
        pred_norm[b : b + 1, :] = square_norms(block_of(pred, table[b, PICK_LANE])) * (UNIT / width)

    def products(b, carry):
        at = slot_row(b, homes)
        mine = jnp.transpose(block_of(pred, table[at, PICK_LANE]))
        for k in range(neighbors_ref.shape[0]):
            other = block_of(true, jnp.minimum(table[at, k], cblocks - 1))
            cost[b * kmax + k] = dot(mine, other, 0) * (2.0 * UNIT / width)
        return carry

    lax.fori_loop(0, slots, products, 0)


def sinkhorn_kernel(
    sizes, table, onehot, cost, pred_norm, true_norm, pred_out, true_out,
    potential, home_cols, spill_cols, pot_cols, tops, sums, spread,
    halves, half_in, merged, parts, share, swap_out, swap_in, last_out, last_in,
    half_send, half_recv, part_send, part_recv, share_send, share_recv, swap_send, swap_recv, last_send, last_recv,
):
    nz, ncol, homes, kmax, log_a, log_b = sizes
    row, col = lax.axis_index("row"), lax.axis_index("col")
    z, core = row // CORES, lax.rem(row, CORES)
    slots = 2 * homes
    cblocks = true_norm.shape[0]
    right, left = lax.rem(col + 1, ncol), lax.rem(col + (ncol - 1), ncol)
    mate = {"row": z * CORES + (1 - core)}
    piece = cblocks // (OWNERS * CORES)
    half = OWNERS * piece

    def far_first(i, n):
        return n // 2 + (1 - 2 * lax.rem(i, 2)) * ((i + 1) // 2)

    def along_z(d, c):
        return {"row": lax.rem(z + d, nz) * CORES + c}

    def ahead(i):
        return jnp.where(i == 0, 1, nz - i)

    def first_block(chip, c):
        return lax.rem(chip, OWNERS) * (CORES * piece) + c * piece

    barrier = pltpu.get_barrier_semaphore()

    def greet(device):
        pl.semaphore_signal(barrier, inc=1, device_id=device, device_id_type=MESH)

    def greet_z(i, carry):
        greet(along_z(i, core))
        return carry

    def greet_col(i, carry):
        greet({"col": lax.rem(col + i, ncol)})
        return carry

    lax.fori_loop(1, nz, greet_z, 0)
    lax.fori_loop(1, ncol, greet_col, 0)
    near = sorted({d % nz for d in (1, -1, 2, -2)})
    for d in near:
        greet(along_z(d, 1 - core))
    greet(mate)
    greeted = nz - 1 + ncol - 1 + len(near) + 1

    for step in range(ITERS):
        potential[step, cblocks : cblocks + TILE, :] = jnp.full((TILE, BLOCK), NEGATIVE, F32)
    home_cols[...] = jnp.zeros((BLOCK, BLOCK), F32)
    spill_cols[...] = jnp.zeros((BLOCK, BLOCK), F32)

    def fill(b, carry):
        tops[b] = jnp.zeros((LISTS, BLOCK), F32)
        sums[b] = jnp.ones((LISTS, BLOCK), F32)
        return carry

    lax.fori_loop(0, slots, fill, 0)
    potential[0, 0:cblocks, :] = -true_norm[...]

    def half_copy(step):
        return pltpu.make_async_remote_copy(
            src_ref=halves.at[step, 1 - core],
            dst_ref=half_in.at[step],
            send_sem=half_send.at[step],
            recv_sem=half_recv.at[step],
            device_id=mate,
            device_id_type=MESH,
        )

    def part_copy(step, i, sending):
        d = far_first(i, nz)
        return pltpu.make_async_remote_copy(
            src_ref=merged.at[step, pl.ds(lax.rem(lax.rem(z + d, nz), OWNERS) * piece, piece)],
            dst_ref=parts.at[step, z if sending else lax.rem(z + (nz - d), nz)],
            send_sem=part_send.at[step, d],
            recv_sem=part_recv.at[step, d],
            device_id=along_z(d, core),
            device_id_type=MESH,
        )

    def share_copy(stage, i, sending):
        d, c = ahead(i // CORES), lax.rem(i, CORES)
        chip, from_core = (z, core) if sending else (lax.rem(z + (nz - d), nz), c)
        return pltpu.make_async_remote_copy(
            src_ref=share.at[stage],
            dst_ref=potential.at[stage, pl.ds(first_block(chip, from_core), piece)],
            send_sem=share_send.at[stage, i],
            recv_sem=share_recv.at[stage, (i - c) + from_core],
            device_id=along_z(d, c),
            device_id_type=MESH,
        )

    def share_mate(stage, sending):
        return pltpu.make_async_remote_copy(
            src_ref=share.at[stage],
            dst_ref=potential.at[stage, pl.ds(first_block(z, core if sending else 1 - core), piece)],
            send_sem=share_send.at[stage, CORES * (OWNERS - 1)],
            recv_sem=share_recv.at[stage, CORES * (OWNERS - 1)],
            device_id=mate,
            device_id_type=MESH,
        )

    def swap_copy(step, spilled):
        return pltpu.make_async_remote_copy(
            src_ref=swap_out.at[step, pl.ds(TILE if spilled else 0, TILE)],
            dst_ref=swap_in.at[step, pl.ds(0 if spilled else TILE, TILE)],
            send_sem=swap_send.at[step, spilled],
            recv_sem=swap_recv.at[step, spilled],
            device_id={"col": left if spilled else right},
            device_id_type=MESH,
        )

    def last_copy(i, sending):
        d = far_first(i, ncol)
        return pltpu.make_async_remote_copy(
            src_ref=last_out,
            dst_ref=last_in.at[pl.ds(TILE * (col if sending else lax.rem(col + (ncol - d), ncol)), TILE)],
            send_sem=last_send.at[d],
            recv_sem=last_recv.at[d],
            device_id={"col": lax.rem(col + d, ncol)},
            device_id_type=MESH,
        )

    def each(count, action):
        def body(i, carry):
            action(i)
            return carry

        lax.fori_loop(0, count, body, 0)

    def iteration(step, carry):
        def over_true(cols):
            def body(b, carry):
                at = slot_row(b, homes)
                near = [potential[step, pl.ds(table[at, k], 1), :] for k in range(kmax)]
                for i in range(BLOCK // ROWS):
                    here = slice(i * ROWS, (i + 1) * ROWS)
                    top, total = top_and_total([cost[b * kmax + k, here, :] + near[k] for k in range(kmax)])
                    high = jnp.max(top, axis=1, keepdims=True)
                    total = jnp.sum(total * jnp.exp2(top - high), axis=1, keepdims=True)
                    cols[here, :] = jnp.where(iota((ROWS, BLOCK), 1) == lax.rem(at, TILE), high + jnp.log2(total), cols[here, :])
                return carry

            return body

        for spilled, cols in ((0, home_cols), (1, spill_cols)):
            lax.fori_loop(spilled * homes, (1 + spilled) * homes, over_true(cols), 0)
            swap_out[step, spilled * TILE : (1 + spilled) * TILE, :] = jnp.transpose(cols[...])[0:TILE, :]
            if not spilled:

                @pl.when(step == 0)
                def _():
                    pl.semaphore_wait(barrier, greeted)

            swap_copy(step, spilled).start()

        def over_pred(b, carry):
            at = lax.rem(slot_row(b, homes), TILE)
            mine = []
            for i in range(BLOCK // TILE):
                held = pot_cols[i * TILE : (i + 1) * TILE, :]
                picked = jnp.sum(jnp.where(iota((TILE, BLOCK), 1) == at, held, 0.0), axis=1, keepdims=True)
                mine.append(jnp.broadcast_to(picked, (TILE, BLOCK)))
            for k in range(kmax):
                top, total = top_and_total(
                    [cost[b * kmax + k, i * TILE : (i + 1) * TILE, :] + mine[i] for i in range(BLOCK // TILE)]
                )
                high = jnp.max(top, axis=0, keepdims=True)
                tops[b, k : k + 1, :] = high
                sums[b, k : k + 1, :] = jnp.sum(total * jnp.exp2(top - high), axis=0, keepdims=True)
            return carry

        for spilled in (1, 0):
            swap_copy(step, 1 - spilled).wait_recv()
            rows = slice(spilled * TILE, (1 + spilled) * TILE)
            pred_rows = log_a - join(swap_out[step, rows, :], swap_in[step, rows, :])
            if not spilled:

                @pl.when(step == ITERS - 1)
                def _():
                    final = (pred_rows + pred_norm[...]) * (1.0 / UNIT)
                    last_out[...] = final
                    last_in[pl.ds(pl.multiple_of(TILE * col, TILE), TILE), :] = final
                    each(ncol - 1, lambda i: last_copy(i, True).start())

            pot_cols[...] = jnp.transpose(jnp.concatenate([pred_rows, jnp.zeros((BLOCK - TILE, BLOCK), F32)], axis=0))
            lax.fori_loop(spilled * homes, (1 + spilled) * homes, over_pred, 0)

        for b in range(slots):
            value = tops[b] + jnp.log2(sums[b])
            first = value.astype(BF16)
            rest = value - first.astype(F32)
            second = rest.astype(BF16)
            third = (rest - second.astype(F32)).astype(BF16)
            none = jnp.where(iota((LISTS, BLOCK), 0) == 0, NEGATIVE, 0.0).astype(BF16)
            spread[b] = dot(onehot[b], jnp.concatenate([first, second, third, none], axis=0), 0)

        def gather(which):
            for g in range(OWNERS):
                top, total = top_and_total(
                    [spread[b, pl.ds(pl.multiple_of(first_block(g, which), piece), piece), :] for b in range(slots)]
                )
                halves[step, which, g * piece : (g + 1) * piece, :] = top + jnp.log2(total)

        gather(1 - core)
        half_copy(step).start()
        gather(core)
        half_copy(step).wait_recv()
        merged[step] = join(halves[step, core], half_in[step])
        each(nz - 1, lambda i: part_copy(step, i, True).start())
        parts[step, z] = merged[step, pl.ds(pl.multiple_of(lax.rem(z, OWNERS) * piece, piece), piece), :]
        each(nz - 1, lambda i: part_copy(step, nz - 2 - i, False).wait_recv())
        top, total = top_and_total([parts[step, i] for i in range(nz)])
        fresh = log_b - (top + jnp.log2(total))
        own = pl.ds(pl.multiple_of(first_block(z, core), piece), piece)
        fresh = jnp.where(step == ITERS - 1, (fresh + true_norm[own, :]) * (1.0 / UNIT), fresh)
        share[step + 1] = fresh
        potential[step + 1, own, :] = fresh
        each(CORES * (OWNERS - 1), lambda i: share_copy(step + 1, CORES * (OWNERS - 1) - 1 - i, True).start())
        share_mate(step + 1, True).start()

        @pl.when(step == ITERS - 1)
        def _():
            each(ncol - 1, lambda i: last_copy(i, False).wait_recv())

            def place(i, carry):
                pred_out[pl.ds(i, 1), :] = last_in[pl.ds(table[2 * TILE, i], 1), :]
                return carry

            lax.fori_loop(0, pred_out.shape[0], place, 0, unroll=8)
            each(ncol - 1, lambda i: last_copy(i, True).wait_send())

        half_copy(step).wait_send()
        for spilled in (0, 1):
            swap_copy(step, spilled).wait_send()
        each(nz - 1, lambda i: part_copy(step, i, True).wait_send())
        share_mate(step + 1, False).wait_recv()
        each(CORES * (OWNERS - 1), lambda i: share_copy(step + 1, i, False).wait_recv())
        return carry

    lax.fori_loop(0, ITERS, iteration, 0)
    true_out[...] = potential[ITERS, 0:cblocks, :]

    def sent(stage, carry):
        each(CORES * (OWNERS - 1), lambda i: share_copy(stage, i, True).wait_send())
        share_mate(stage, True).wait_send()
        return carry

    lax.fori_loop(1, ITERS + 1, sent, 0)


def on_device(pred_feat, true_feat, neighbors, counts):
    width = pred_feat.shape[1]
    rblocks, cblocks = pred_feat.shape[0] // BLOCK, true_feat.shape[0] // BLOCK
    nrow, ncol = lax.axis_size("row"), lax.axis_size("col")
    nz, homes, kmax = nrow // CORES, rblocks // ncol, neighbors.shape[2]
    slots, half = 2 * homes, cblocks // CORES
    piece = half // OWNERS
    log_a = -math.log2(pred_feat.shape[0] * nrow)
    log_b = -math.log2(true_feat.shape[0] * ncol)
    vmem = pl.BlockSpec(memory_space=pltpu.VMEM)
    anywhere = pl.BlockSpec(memory_space=pl.ANY)
    dma = pltpu.SemaphoreType.DMA
    ready = pl.pallas_call(
        functools.partial(prepare_kernel, ncol, homes),
        out_shape=(
            jax.ShapeDtypeStruct((3 * TILE, BLOCK), I32),
            jax.ShapeDtypeStruct((slots, cblocks, 4 * LISTS), BF16),
            jax.ShapeDtypeStruct((slots * kmax, BLOCK, BLOCK), F32),
            jax.ShapeDtypeStruct((TILE, BLOCK), F32),
            jax.ShapeDtypeStruct((cblocks, BLOCK), F32),
        ),
        in_specs=[vmem, vmem, anywhere, anywhere],
        out_specs=(vmem,) * 5,
        scratch_shapes=[
            pltpu.VMEM((width, rblocks * BLOCK), BF16),
            pltpu.VMEM((width, cblocks * BLOCK), BF16),
            pltpu.SMEM((3 * TILE, BLOCK), I32),
            dma((3,)),
        ],
        compiler_params=pltpu.CompilerParams(vmem_limit_bytes=24 * 2**20),
        name="prepare",
    )(counts.T, jnp.transpose(neighbors, (2, 1, 0)), pred_feat.T, true_feat.T)
    pred_pot, true_pot = pl.pallas_call(
        functools.partial(sinkhorn_kernel, (nz, ncol, homes, kmax, log_a, log_b)),
        out_shape=(
            jax.ShapeDtypeStruct((rblocks, BLOCK), F32),
            jax.ShapeDtypeStruct((cblocks, BLOCK), F32),
        ),
        in_specs=[
            pl.BlockSpec(memory_space=pltpu.SMEM),
            vmem,
            vmem,
            vmem,
            vmem,
        ],
        out_specs=(vmem, vmem),
        scratch_shapes=[
            pltpu.VMEM((ITERS + 1, cblocks + TILE, BLOCK), F32),
            pltpu.VMEM((BLOCK, BLOCK), F32),
            pltpu.VMEM((BLOCK, BLOCK), F32),
            pltpu.VMEM((BLOCK, BLOCK), F32),
            pltpu.VMEM((slots, LISTS, BLOCK), F32),
            pltpu.VMEM((slots, LISTS, BLOCK), F32),
            pltpu.VMEM((slots, cblocks, BLOCK), F32),
            pltpu.VMEM((ITERS, CORES, half, BLOCK), F32),
            pltpu.VMEM((ITERS, half, BLOCK), F32),
            pltpu.VMEM((ITERS, half, BLOCK), F32),
            pltpu.VMEM((ITERS, nz, piece, BLOCK), F32),
            pltpu.VMEM((ITERS + 1, piece, BLOCK), F32),
            pltpu.VMEM((ITERS, 2 * TILE, BLOCK), F32),
            pltpu.VMEM((ITERS, 2 * TILE, BLOCK), F32),
            pltpu.VMEM((TILE, BLOCK), F32),
            pltpu.VMEM((TILE * ncol, BLOCK), F32),
            dma((ITERS,)),
            dma((ITERS,)),
            dma((ITERS, nz)),
            dma((ITERS, nz)),
            dma((ITERS + 1, CORES * (OWNERS - 1) + 1)),
            dma((ITERS + 1, CORES * (OWNERS - 1) + 1)),
            dma((ITERS, 2)),
            dma((ITERS, 2)),
            dma((ncol,)),
            dma((ncol,)),
        ],
        compiler_params=pltpu.CompilerParams(
            collective_id=0, has_side_effects=True, vmem_limit_bytes=24 * 2**20
        ),
        name="sinkhorn",
    )(*ready)
    return (pred_pot.reshape(-1), true_pot.reshape(-1))


def solution(mesh):
    in_specs = (P("row", None), P("col", None), P("row", "col", None), P("row", None))
    out_specs = (P("row"), P("col"))
    return jax.shard_map(
        on_device, mesh=mesh, in_specs=in_specs, out_specs=out_specs, check_vma=False
    )
```

time: 129 us -> 96.7 us (0.75)
  Pallas kernels: 123 us -> 90.3 us
    pallas_call x1, Pallas kernels: 117 us -> 84.8 us  [on_device(): pl.pallas_call(functools.partial(sinkhorn_kernel, (nz, ncol, homes, kmax,...]
where the time goes in v2:
time: 96.7 us; the launch traced here: 96.5 us
  Pallas kernels  90.3 us (93%)
  local copies, waits for them, and re-layouts  5.54 us (6%)
    pallas_call x1, Pallas kernels, on_device(): pl.pallas_call(functools.partial(sinkhorn_kernel, (nz, ncol, homes, kmax,...  84.8 us
    unnamed x10, local copies, waits for them, and re-layouts  5.54 us
    pallas_call x1, Pallas kernels, on_device(): pl.pallas_call(functools.partial(prepare_kernel, ncol, homes), out_shape=...  5.48 us

profile of v2, /device:TPU:1, one launch (start us, length us, event | category | flops | bytes accessed | tf_op | source)
XLA Modules:
  0.0 96.5 jit_solution(1413742714475926257)
XLA Ops:
  0.6 0.0 copy-start
  0.6 1.6 %copy-done = bf16[16384,64]{0,1:T(8,128)(2,1)S(1)} copy-done((bf16[16384,64]{0,1:T(8,128)(2,1)S(1)}, bf16[16384,64]{0,1:T(8,128)(2,1)}, u32[]{:S(2)}) %copy-start) | copy-done | bytes 2097176
  2.2 0.0 copy-start.1
  2.2 1.3 %copy-done.1 = bf16[10240,64]{0,1:T(8,128)(2,1)S(1)} copy-done((bf16[10240,64]{0,1:T(8,128)(2,1)S(1)}, bf16[10240,64]{0,1:T(8,128)(2,1)}, u32[]{:S(2)}) %copy-start.1) | copy-done | bytes 1310744
  3.5 0.0 copy-start.2
  3.5 0.7 copy-done.2
  4.2 0.0 copy-start.3
  4.2 0.7 copy-done.3
  4.9 5.5 %prepare.1 = (s32[24,128]{1,0:T(8,128)S(1)}, bf16[10,128,64]{2,1,0:T(8,128)(2,1)S(1)}, f32[120,128,128]{2,1,0:T(8,128)S(1)}, f32[8,128]{1,0:T(8,128)S(1)}, f32[128,128]{1,0:T(8,128)S(1)}) custom-call(s32[16,80]{1,0:T(8,128)S(1)} %bitcast.10, s32[12,1,80]{2,1,0:T(1,128)S(1)} %bitcast.11, bf16[64,10240]{1,0:T(8,128)(2,1)S(1)} %bitcast.7, ...), custom_call_target="tpu_custom_call" | custom-call | tf_op jit(solution)/shard_map/prepare/pallas_call | solution.py:405
  10.4 84.8 %sinkhorn.1 = (f32[80,128]{1,0:T(8,128)S(1)}, f32[128,128]{1,0:T(8,128)S(1)}) custom-call(s32[24,128]{1,0:T(8,128)S(1)} %get-tuple-element.9.table, bf16[10,128,64]{2,1,0:T(8,128)(2,1)S(1)} %get-tuple-element.10.onehot, f32[120,128,128]{2,1,0:T(8,128)S(1)} %get-tuple-element.11.cost, f32[8,128]{1,0:T(8,128)S(1)} %get-tuple-element.12.pred_norm, ...), custom_call_target="tpu_custom_call" | custom-call | tf_op jit(solution)/shard_map/sinkhorn/pallas_call | solution.py:425
  95.2 0.6 copy.8
  95.8 0.6 copy.9
Async XLA Ops:
  0.6 1.6 %copy-start = (bf16[16384,64]{0,1:T(8,128)(2,1)S(1)}, bf16[16384,64]{0,1:T(8,128)(2,1)}, u32[]{:S(2)}) copy-start(bf16[16384,64]{0,1:T(8,128)(2,1)} %param.5) | copy-start | bytes 6291460
  2.2 1.3 %copy-start.1 = (bf16[10240,64]{0,1:T(8,128)(2,1)S(1)}, bf16[10240,64]{0,1:T(8,128)(2,1)}, u32[]{:S(2)}) copy-start(bf16[10240,64]{0,1:T(8,128)(2,1)} %param.4) | copy-start | bytes 3932164
  3.5 0.7 copy-start.2
  4.2 0.7 copy-start.3

commit v3 on v2

--- a/solution.py
+++ b/solution.py
@@ -62,18 +62,12 @@
 
 
 def prepare_kernel(
-    ncol, homes, counts_ref, neighbors_ref, pred_hbm, true_hbm, table_ref, onehot, cost, pred_norm, true_norm,
-    pred, true, table, load_sem,
+    ncol, homes, counts_ref, neighbors_ref, pred, true, table_ref, onehot, cost, pred_norm, true_norm,
+    table, copied,
 ):
     here = lax.axis_index("col")
     width, cblocks = true.shape[0], true_norm.shape[0]
     slots = 2 * homes
-    loads = [
-        pltpu.make_async_copy(true_hbm, true, load_sem.at[0]),
-        pltpu.make_async_copy(pred_hbm, pred, load_sem.at[1]),
-    ]
-    for load in loads:
-        load.start()
     counts = counts_ref[...].astype(F32)
     blocks, kmax = counts.shape[1], neighbors_ref.shape[0]
     to, frm = iota((ncol, ncol), 0), iota((ncol, ncol), 1)
@@ -99,7 +93,7 @@
     table_ref[0 : 2 * TILE, :] = found.astype(I32)
     table_ref[2 * TILE : 3 * TILE, :] = jnp.zeros((TILE, BLOCK), I32)
     table_ref[2 * TILE : 2 * TILE + 1, 0:blocks] = place.astype(I32)
-    to_scalar = pltpu.make_async_copy(table_ref, table, load_sem.at[2])
+    to_scalar = pltpu.make_async_copy(table_ref, table, copied)
     to_scalar.start()
 
     def match_blocks(b, carry):
@@ -112,14 +106,11 @@
 
     lax.fori_loop(0, slots, match_blocks, 0)
 
-    loads[0].wait()
-
     def norm_row(i, carry):
         true_norm[pl.ds(i, 1), :] = square_norms(block_of(true, i)) * (UNIT / width)
         return carry
 
     lax.fori_loop(0, cblocks, norm_row, 0, unroll=8)
-    loads[1].wait()
     to_scalar.wait()
     pred_norm[...] = jnp.zeros((TILE, BLOCK), F32)
     for b in range(homes):
@@ -138,7 +129,7 @@
 
 def sinkhorn_kernel(
     sizes, table, onehot, cost, pred_norm, true_norm, pred_out, true_out,
-    potential, home_cols, spill_cols, pot_cols, tops, sums, spread,
+    potential, held, tops, sums, spread,
     halves, half_in, merged, parts, share, swap_out, swap_in, last_out, last_in,
     half_send, half_recv, part_send, part_recv, share_send, share_recv, swap_send, swap_recv, last_send, last_recv,
 ):
@@ -187,15 +178,9 @@
 
     for step in range(ITERS):
         potential[step, cblocks : cblocks + TILE, :] = jnp.full((TILE, BLOCK), NEGATIVE, F32)
-    home_cols[...] = jnp.zeros((BLOCK, BLOCK), F32)
-    spill_cols[...] = jnp.zeros((BLOCK, BLOCK), F32)
-
-    def fill(b, carry):
-        tops[b] = jnp.zeros((LISTS, BLOCK), F32)
-        sums[b] = jnp.ones((LISTS, BLOCK), F32)
-        return carry
-
-    lax.fori_loop(0, slots, fill, 0)
+    swap_out[...] = jnp.zeros(swap_out.shape, F32)
+    tops[...] = jnp.zeros(tops.shape, F32)
+    sums[...] = jnp.ones(sums.shape, F32)
     potential[0, 0:cblocks, :] = -true_norm[...]
 
     def half_copy(step):
@@ -270,23 +255,18 @@
         lax.fori_loop(0, count, body, 0)
 
     def iteration(step, carry):
-        def over_true(cols):
-            def body(b, carry):
-                at = slot_row(b, homes)
+        for spilled in (0, 1):
+            for b in range(spilled * homes, (1 + spilled) * homes):
+                at = b if b < homes else b + (TILE - homes)
                 near = [potential[step, pl.ds(table[at, k], 1), :] for k in range(kmax)]
-                for i in range(BLOCK // ROWS):
-                    here = slice(i * ROWS, (i + 1) * ROWS)
-                    top, total = top_and_total([cost[b * kmax + k, here, :] + near[k] for k in range(kmax)])
-                    high = jnp.max(top, axis=1, keepdims=True)
-                    total = jnp.sum(total * jnp.exp2(top - high), axis=1, keepdims=True)
-                    cols[here, :] = jnp.where(iota((ROWS, BLOCK), 1) == lax.rem(at, TILE), high + jnp.log2(total), cols[here, :])
-                return carry
-
-            return body
-
-        for spilled, cols in ((0, home_cols), (1, spill_cols)):
-            lax.fori_loop(spilled * homes, (1 + spilled) * homes, over_true(cols), 0)
-            swap_out[step, spilled * TILE : (1 + spilled) * TILE, :] = jnp.transpose(cols[...])[0:TILE, :]
+                found = [
+                    top_and_total([cost[b * kmax + k, i : i + ROWS, :] + near[k] for k in range(kmax)])
+                    for i in range(0, BLOCK, ROWS)
+                ]
+                top, total = (jnp.transpose(jnp.concatenate(part, axis=0)) for part in zip(*found))
+                high = jnp.max(top, axis=0, keepdims=True)
+                total = jnp.sum(total * jnp.exp2(top - high), axis=0, keepdims=True)
+                swap_out[step, at : at + 1, :] = high + jnp.log2(total)
             if not spilled:
 
                 @pl.when(step == 0)
@@ -296,15 +276,12 @@
             swap_copy(step, spilled).start()
 
         def over_pred(b, carry):
-            at = lax.rem(slot_row(b, homes), TILE)
-            mine = []
-            for i in range(BLOCK // TILE):
-                held = pot_cols[i * TILE : (i + 1) * TILE, :]
-                picked = jnp.sum(jnp.where(iota((TILE, BLOCK), 1) == at, held, 0.0), axis=1, keepdims=True)
-                mine.append(jnp.broadcast_to(picked, (TILE, BLOCK)))
             for k in range(kmax):
                 top, total = top_and_total(
-                    [cost[b * kmax + k, i * TILE : (i + 1) * TILE, :] + mine[i] for i in range(BLOCK // TILE)]
+                    [
+                        cost[b * kmax + k, i : i + TILE, :] + held[lax.rem(b, homes), i : i + TILE, :]
+                        for i in range(0, BLOCK, TILE)
+                    ]
                 )
                 high = jnp.max(top, axis=0, keepdims=True)
                 tops[b, k : k + 1, :] = high
@@ -324,7 +301,9 @@
                     last_in[pl.ds(pl.multiple_of(TILE * col, TILE), TILE), :] = final
                     each(ncol - 1, lambda i: last_copy(i, True).start())
 
-            pot_cols[...] = jnp.transpose(jnp.concatenate([pred_rows, jnp.zeros((BLOCK - TILE, BLOCK), F32)], axis=0))
+            across = jnp.transpose(jnp.concatenate([pred_rows, jnp.zeros((BLOCK - TILE, BLOCK), F32)], axis=0))
+            for b in range(homes):
+                held[b] = jnp.broadcast_to(across[:, b : b + 1], (BLOCK, BLOCK))
             lax.fori_loop(spilled * homes, (1 + spilled) * homes, over_pred, 0)
 
         for b in range(slots):
@@ -400,7 +379,6 @@
     log_a = -math.log2(pred_feat.shape[0] * nrow)
     log_b = -math.log2(true_feat.shape[0] * ncol)
     vmem = pl.BlockSpec(memory_space=pltpu.VMEM)
-    anywhere = pl.BlockSpec(memory_space=pl.ANY)
     dma = pltpu.SemaphoreType.DMA
     ready = pl.pallas_call(
         functools.partial(prepare_kernel, ncol, homes),
@@ -411,13 +389,11 @@
             jax.ShapeDtypeStruct((TILE, BLOCK), F32),
             jax.ShapeDtypeStruct((cblocks, BLOCK), F32),
         ),
-        in_specs=[vmem, vmem, anywhere, anywhere],
+        in_specs=[vmem] * 4,
         out_specs=(vmem,) * 5,
         scratch_shapes=[
-            pltpu.VMEM((width, rblocks * BLOCK), BF16),
-            pltpu.VMEM((width, cblocks * BLOCK), BF16),
             pltpu.SMEM((3 * TILE, BLOCK), I32),
-            dma((3,)),
+            dma(()),
         ],
         compiler_params=pltpu.CompilerParams(vmem_limit_bytes=24 * 2**20),
         name="prepare",
@@ -438,9 +414,7 @@
         out_specs=(vmem, vmem),
         scratch_shapes=[
             pltpu.VMEM((ITERS + 1, cblocks + TILE, BLOCK), F32),
-            pltpu.VMEM((BLOCK, BLOCK), F32),
-            pltpu.VMEM((BLOCK, BLOCK), F32),
-            pltpu.VMEM((BLOCK, BLOCK), F32),
+            pltpu.VMEM((homes, BLOCK, BLOCK), F32),
             pltpu.VMEM((slots, LISTS, BLOCK), F32),
             pltpu.VMEM((slots, LISTS, BLOCK), F32),
             pltpu.VMEM((slots, cblocks, BLOCK), F32),

time: 96.7 us -> 92.9 us (0.961)
  Pallas kernels: 90.3 us -> 86.4 us
    pallas_call x1, Pallas kernels: 84.8 us -> 81.2 us  [on_device(): pl.pallas_call(functools.partial(sinkhorn_kernel, (nz, ncol, homes, kmax,...]
where the time goes in v3:
time: 92.9 us; the launch traced here: 92.6 us
  Pallas kernels  86.4 us (93%)
  local copies, waits for them, and re-layouts  5.54 us (6%)
    pallas_call x1, Pallas kernels, on_device(): pl.pallas_call(functools.partial(sinkhorn_kernel, (nz, ncol, homes, kmax,...  81.2 us
    unnamed x10, local copies, waits for them, and re-layouts  5.54 us
    pallas_call x1, Pallas kernels, on_device(): pl.pallas_call(functools.partial(prepare_kernel, ncol, homes), out_shape=...  5.23 us

profile of v3, /device:TPU:1, one launch (start us, length us, event | category | flops | bytes accessed | tf_op | source)
XLA Modules:
  0.0 92.6 jit_solution(12183155483984340815)
XLA Ops:
  0.6 0.0 copy-start
  0.6 1.6 %copy-done = bf16[16384,64]{0,1:T(8,128)(2,1)S(1)} copy-done((bf16[16384,64]{0,1:T(8,128)(2,1)S(1)}, bf16[16384,64]{0,1:T(8,128)(2,1)}, u32[]{:S(2)}) %copy-start) | copy-done | bytes 2097176
  2.2 0.0 copy-start.1
  2.2 1.3 %copy-done.1 = bf16[10240,64]{0,1:T(8,128)(2,1)S(1)} copy-done((bf16[10240,64]{0,1:T(8,128)(2,1)S(1)}, bf16[10240,64]{0,1:T(8,128)(2,1)}, u32[]{:S(2)}) %copy-start.1) | copy-done | bytes 1310744
  3.5 0.0 copy-start.2
  3.5 0.7 copy-done.2
  4.2 0.0 copy-start.3
  4.2 0.7 copy-done.3
  4.9 5.2 %prepare.1 = (s32[24,128]{1,0:T(8,128)S(1)}, bf16[10,128,64]{2,1,0:T(8,128)(2,1)S(1)}, f32[120,128,128]{2,1,0:T(8,128)S(1)}, f32[8,128]{1,0:T(8,128)S(1)}, f32[128,128]{1,0:T(8,128)S(1)}) custom-call(s32[16,80]{1,0:T(8,128)S(1)} %bitcast.10, s32[12,1,80]{2,1,0:T(1,128)S(1)} %bitcast.11, bf16[64,10240]{1,0:T(8,128)(2,1)S(1)} %bitcast.7, ...), custom_call_target="tpu_custom_call" | custom-call | tf_op jit(solution)/shard_map/prepare/pallas_call | solution.py:383
  10.2 81.2 %sinkhorn.1 = (f32[80,128]{1,0:T(8,128)S(1)}, f32[128,128]{1,0:T(8,128)S(1)}) custom-call(s32[24,128]{1,0:T(8,128)S(1)} %get-tuple-element.9.table, bf16[10,128,64]{2,1,0:T(8,128)(2,1)S(1)} %get-tuple-element.10.onehot, f32[120,128,128]{2,1,0:T(8,128)S(1)} %get-tuple-element.11.cost, f32[8,128]{1,0:T(8,128)S(1)} %get-tuple-element.12.pred_norm, ...), custom_call_target="tpu_custom_call" | custom-call | tf_op jit(solution)/shard_map/sinkhorn/pallas_call | solution.py:401
  91.3 0.6 copy.8
  92.0 0.6 copy.9
Async XLA Ops:
  0.6 1.6 %copy-start = (bf16[16384,64]{0,1:T(8,128)(2,1)S(1)}, bf16[16384,64]{0,1:T(8,128)(2,1)}, u32[]{:S(2)}) copy-start(bf16[16384,64]{0,1:T(8,128)(2,1)} %param.5) | copy-start | bytes 6291460
  2.2 1.3 %copy-start.1 = (bf16[10240,64]{0,1:T(8,128)(2,1)S(1)}, bf16[10240,64]{0,1:T(8,128)(2,1)}, u32[]{:S(2)}) copy-start(bf16[10240,64]{0,1:T(8,128)(2,1)} %param.4) | copy-start | bytes 3932164
  3.5 0.7 copy-start.2
  4.2 0.7 copy-start.3

commit v4 on v3

--- a/solution.py
+++ b/solution.py
@@ -53,21 +53,13 @@
     return jnp.sum(wide * wide, axis=0, keepdims=True)
 
 
-def block_of(features, index):
-    return features[:, pl.ds(pl.multiple_of(BLOCK * index, BLOCK), BLOCK)]
-
-
 def slot_row(b, homes):
-    return jnp.where(b < homes, b, b + (TILE - homes))
-
-
-def prepare_kernel(
-    ncol, homes, counts_ref, neighbors_ref, pred, true, table_ref, onehot, cost, pred_norm, true_norm,
-    table, copied,
-):
+    return b if b < homes else b + (TILE - homes)
+
+
+def prepare_kernel(ncol, homes, counts_ref, neighbors_ref, table_ref, onehot):
     here = lax.axis_index("col")
-    width, cblocks = true.shape[0], true_norm.shape[0]
-    slots = 2 * homes
+    cblocks = onehot.shape[1]
     counts = counts_ref[...].astype(F32)
     blocks, kmax = counts.shape[1], neighbors_ref.shape[0]
     to, frm = iota((ncol, ncol), 0), iota((ncol, ncol), 1)
@@ -93,51 +85,30 @@
     table_ref[0 : 2 * TILE, :] = found.astype(I32)
     table_ref[2 * TILE : 3 * TILE, :] = jnp.zeros((TILE, BLOCK), I32)
     table_ref[2 * TILE : 2 * TILE + 1, 0:blocks] = place.astype(I32)
-    to_scalar = pltpu.make_async_copy(table_ref, table, copied)
-    to_scalar.start()
-
-    def match_blocks(b, carry):
-        listed = table_ref[pl.ds(slot_row(b, homes), 1), 0 : 4 * LISTS]
+    first_named = jnp.where(lane == PICK_LANE, pick, jnp.where(live, listed, 0.0))
+    table_ref[3 * TILE : 5 * TILE, :] = first_named.astype(I32)
+
+    for b in range(2 * homes):
+        at = slot_row(b, homes)
+        listed = table_ref[at : at + 1, 0 : 4 * LISTS]
         lane = iota((cblocks, 4 * LISTS), 1)
         match = ((iota((cblocks, 4 * LISTS), 0) == listed) & (lane < 3 * LISTS)).astype(F32)
         absent = 1.0 - jnp.sum(jnp.where(lane < LISTS, match, 0.0), axis=1, keepdims=True)
         onehot[b] = jnp.where(lane == 3 * LISTS, absent, match).astype(BF16)
-        return carry
-
-    lax.fori_loop(0, slots, match_blocks, 0)
-
-    def norm_row(i, carry):
-        true_norm[pl.ds(i, 1), :] = square_norms(block_of(true, i)) * (UNIT / width)
-        return carry
-
-    lax.fori_loop(0, cblocks, norm_row, 0, unroll=8)
-    to_scalar.wait()
-    pred_norm[...] = jnp.zeros((TILE, BLOCK), F32)
-    for b in range(homes):
-        pred_norm[b : b + 1, :] = square_norms(block_of(pred, table[b, PICK_LANE])) * (UNIT / width)
-
-    def products(b, carry):
-        at = slot_row(b, homes)
-        mine = jnp.transpose(block_of(pred, table[at, PICK_LANE]))
-        for k in range(neighbors_ref.shape[0]):
-            other = block_of(true, jnp.minimum(table[at, k], cblocks - 1))
-            cost[b * kmax + k] = dot(mine, other, 0) * (2.0 * UNIT / width)
-        return carry
-
-    lax.fori_loop(0, slots, products, 0)
 
 
 def sinkhorn_kernel(
-    sizes, table, onehot, cost, pred_norm, true_norm, pred_out, true_out,
+    sizes, table, onehot_hbm, pred_hbm, true_hbm, pred_out, true_out,
+    pred, true, pred_blocks, true_blocks, onehot, cost, pred_norm, true_norm,
     potential, held, tops, sums, spread,
     halves, half_in, merged, parts, share, swap_out, swap_in, last_out, last_in,
-    half_send, half_recv, part_send, part_recv, share_send, share_recv, swap_send, swap_recv, last_send, last_recv,
+    load_sem, half_send, half_recv, part_send, part_recv, share_send, share_recv, swap_send, swap_recv, last_send, last_recv,
 ):
     nz, ncol, homes, kmax, log_a, log_b = sizes
     row, col = lax.axis_index("row"), lax.axis_index("col")
     z, core = row // CORES, lax.rem(row, CORES)
     slots = 2 * homes
-    cblocks = true_norm.shape[0]
+    cblocks, width = true_norm.shape[0], true.shape[0]
     right, left = lax.rem(col + 1, ncol), lax.rem(col + (ncol - 1), ncol)
     mate = {"row": z * CORES + (1 - core)}
     piece = cblocks // (OWNERS * CORES)
@@ -154,6 +125,14 @@
 
     def first_block(chip, c):
         return lax.rem(chip, OWNERS) * (CORES * piece) + c * piece
+
+    loads = [
+        pltpu.make_async_copy(true_hbm, true, load_sem.at[0]),
+        pltpu.make_async_copy(pred_hbm, pred, load_sem.at[1]),
+        pltpu.make_async_copy(onehot_hbm, onehot, load_sem.at[2]),
+    ]
+    for load in loads:
+        load.start()
 
     barrier = pltpu.get_barrier_semaphore()
 
@@ -181,7 +160,36 @@
     swap_out[...] = jnp.zeros(swap_out.shape, F32)
     tops[...] = jnp.zeros(tops.shape, F32)
     sums[...] = jnp.ones(sums.shape, F32)
+    pred_norm[...] = jnp.zeros(pred_norm.shape, F32)
+    loads[0].wait()
+
+    def take_true(i, carry):
+        block = true[:, pl.ds(pl.multiple_of(BLOCK * i, BLOCK), BLOCK)]
+        true_blocks[i] = block
+        true_norm[pl.ds(i, 1), :] = square_norms(block) * (UNIT / width)
+        return carry
+
+    lax.fori_loop(0, cblocks, take_true, 0, unroll=16)
     potential[0, 0:cblocks, :] = -true_norm[...]
+    loads[1].wait()
+
+    def take_pred(i, carry):
+        pred_blocks[i] = pred[:, pl.ds(pl.multiple_of(BLOCK * i, BLOCK), BLOCK)]
+        return carry
+
+    lax.fori_loop(0, pred_out.shape[0], take_pred, 0, unroll=16)
+    loads[2].wait()
+    for b in range(homes):
+        pred_norm[b : b + 1, :] = square_norms(pred_blocks[table[b, PICK_LANE]]) * (UNIT / width)
+
+    def products(b, carry):
+        at = 3 * TILE + jnp.where(b < homes, b, b + (TILE - homes))
+        mine = jnp.transpose(pred_blocks[table[at, PICK_LANE]])
+        for k in range(kmax):
+            cost[b * kmax + k] = dot(mine, true_blocks[table[at, k]], 0) * (2.0 * UNIT / width)
+        return carry
+
+    lax.fori_loop(0, slots, products, 0)
 
     def half_copy(step):
         return pltpu.make_async_remote_copy(
@@ -257,7 +265,7 @@
     def iteration(step, carry):
         for spilled in (0, 1):
             for b in range(spilled * homes, (1 + spilled) * homes):
-                at = b if b < homes else b + (TILE - homes)
+                at = slot_row(b, homes)
                 near = [potential[step, pl.ds(table[at, k], 1), :] for k in range(kmax)]
                 found = [
                     top_and_total([cost[b * kmax + k, i : i + ROWS, :] + near[k] for k in range(kmax)])
@@ -379,40 +387,36 @@
     log_a = -math.log2(pred_feat.shape[0] * nrow)
     log_b = -math.log2(true_feat.shape[0] * ncol)
     vmem = pl.BlockSpec(memory_space=pltpu.VMEM)
+    hbm = pl.BlockSpec(memory_space=pl.ANY)
     dma = pltpu.SemaphoreType.DMA
     ready = pl.pallas_call(
         functools.partial(prepare_kernel, ncol, homes),
         out_shape=(
-            jax.ShapeDtypeStruct((3 * TILE, BLOCK), I32),
+            jax.ShapeDtypeStruct((5 * TILE, BLOCK), I32),
             jax.ShapeDtypeStruct((slots, cblocks, 4 * LISTS), BF16),
-            jax.ShapeDtypeStruct((slots * kmax, BLOCK, BLOCK), F32),
-            jax.ShapeDtypeStruct((TILE, BLOCK), F32),
-            jax.ShapeDtypeStruct((cblocks, BLOCK), F32),
         ),
-        in_specs=[vmem] * 4,
-        out_specs=(vmem,) * 5,
-        scratch_shapes=[
-            pltpu.SMEM((3 * TILE, BLOCK), I32),
-            dma(()),
-        ],
-        compiler_params=pltpu.CompilerParams(vmem_limit_bytes=24 * 2**20),
+        in_specs=[vmem, vmem],
+        out_specs=(vmem, vmem),
+        compiler_params=pltpu.CompilerParams(vmem_limit_bytes=60 * 2**20),
         name="prepare",
-    )(counts.T, jnp.transpose(neighbors, (2, 1, 0)), pred_feat.T, true_feat.T)
+    )(counts.T, jnp.transpose(neighbors, (2, 1, 0)))
     pred_pot, true_pot = pl.pallas_call(
         functools.partial(sinkhorn_kernel, (nz, ncol, homes, kmax, log_a, log_b)),
         out_shape=(
             jax.ShapeDtypeStruct((rblocks, BLOCK), F32),
             jax.ShapeDtypeStruct((cblocks, BLOCK), F32),
         ),
-        in_specs=[
-            pl.BlockSpec(memory_space=pltpu.SMEM),
-            vmem,
-            vmem,
-            vmem,
-            vmem,
-        ],
+        in_specs=[pl.BlockSpec(memory_space=pltpu.SMEM), hbm, hbm, hbm],
         out_specs=(vmem, vmem),
         scratch_shapes=[
+            pltpu.VMEM((width, rblocks * BLOCK), BF16),
+            pltpu.VMEM((width, cblocks * BLOCK), BF16),
+            pltpu.VMEM((rblocks, width, BLOCK), BF16),
+            pltpu.VMEM((cblocks, width, BLOCK), BF16),
+            pltpu.VMEM((slots, cblocks, 4 * LISTS), BF16),
+            pltpu.VMEM((slots * kmax, BLOCK, BLOCK), F32),
+            pltpu.VMEM((TILE, BLOCK), F32),
+            pltpu.VMEM((cblocks, BLOCK), F32),
             pltpu.VMEM((ITERS + 1, cblocks + TILE, BLOCK), F32),
             pltpu.VMEM((homes, BLOCK, BLOCK), F32),
             pltpu.VMEM((slots, LISTS, BLOCK), F32),
@@ -427,6 +431,7 @@
             pltpu.VMEM((ITERS, 2 * TILE, BLOCK), F32),
             pltpu.VMEM((TILE, BLOCK), F32),
             pltpu.VMEM((TILE * ncol, BLOCK), F32),
+            dma((3,)),
             dma((ITERS,)),
             dma((ITERS,)),
             dma((ITERS, nz)),
@@ -439,10 +444,10 @@
             dma((ncol,)),
         ],
         compiler_params=pltpu.CompilerParams(
-            collective_id=0, has_side_effects=True, vmem_limit_bytes=24 * 2**20
+            collective_id=0, has_side_effects=True, vmem_limit_bytes=60 * 2**20
         ),
         name="sinkhorn",
-    )(*ready)
+    )(*ready, pred_feat.T, true_feat.T)
     return (pred_pot.reshape(-1), true_pot.reshape(-1))
 
 

time: 92.9 us -> 89.5 us (0.963)
  local copies, waits for them, and re-layouts: 5.54 us -> 2.87 us
    pallas_call x1, Pallas kernels: 5.23 us -> 2.16 us  [on_device(): pl.pallas_call(functools.partial(prepare_kernel, ncol, homes), out_shape=...]
    unnamed x10 -> x2, local copies, waits for them, and re-layouts: 5.54 us -> 2.87 us
    pallas_call x1, Pallas kernels: 81.2 us -> 83.5 us  [on_device(): pl.pallas_call(functools.partial(sinkhorn_kernel, (nz, ncol, homes, kmax,...]
where the time goes in v4:
time: 89.5 us; the launch traced here: 89.1 us
  Pallas kernels  85.6 us (96%)
  local copies, waits for them, and re-layouts  2.87 us (3%)
    pallas_call x1, Pallas kernels, on_device(): pl.pallas_call(functools.partial(sinkhorn_kernel, (nz, ncol, homes, kmax,...  83.5 us
    unnamed x2, local copies, waits for them, and re-layouts  2.87 us
    pallas_call x1, Pallas kernels, on_device(): pl.pallas_call(functools.partial(prepare_kernel, ncol, homes), out_shape=...  2.16 us

profile of v4, /device:TPU:1, one launch (start us, length us, event | category | flops | bytes accessed | tf_op | source)
XLA Modules:
  0.0 89.1 jit_solution(16991398784839117615)
XLA Ops:
  0.6 2.2 %prepare.1 = (s32[40,128]{1,0:T(8,128)}, bf16[10,128,64]{2,1,0:T(8,128)(2,1)}) custom-call(s32[16,80]{1,0:T(8,128)} %bitcast.10, s32[12,1,80]{2,1,0:T(1,128)} %bitcast.11), custom_call_target="tpu_custom_call" | custom-call | tf_op jit(solution)/shard_map/prepare/pallas_call | solution.py:392
  2.8 83.5 %sinkhorn.1 = (f32[80,128]{1,0:T(8,128)}, f32[128,128]{1,0:T(8,128)}) custom-call(s32[40,128]{1,0:T(8,128)} %get-tuple-element.6.table, bf16[10,128,64]{2,1,0:T(8,128)(2,1)} %get-tuple-element.7.onehot_hbm, bf16[64,10240]{1,0:T(8,128)(2,1)} %bitcast.7, bf16[64,16384]{1,0:T(8,128)(2,1)} %bitcast.6), custom_call_target="tpu_custom_call" | custom-call | tf_op jit(solution)/shard_map/sinkhorn/pallas_call | solution.py:403
  86.3 1.4 %copy.8 = f32[10240]{0:T(1024)} copy(f32[10240]{0:T(1024)} %bitcast.9) | data formatting | bytes 81920
  87.7 1.5 %copy.9 = f32[16384]{0:T(1024)} copy(f32[16384]{0:T(1024)} %bitcast.8) | data formatting | bytes 131072

commit v5 on v4

--- a/solution.py
+++ b/solution.py
@@ -397,7 +397,7 @@
         ),
         in_specs=[vmem, vmem],
         out_specs=(vmem, vmem),
-        compiler_params=pltpu.CompilerParams(vmem_limit_bytes=60 * 2**20),
+        compiler_params=pltpu.CompilerParams(vmem_limit_bytes=53 * 2**20),
         name="prepare",
     )(counts.T, jnp.transpose(neighbors, (2, 1, 0)))
     pred_pot, true_pot = pl.pallas_call(
@@ -444,7 +444,7 @@
             dma((ncol,)),
         ],
         compiler_params=pltpu.CompilerParams(
-            collective_id=0, has_side_effects=True, vmem_limit_bytes=60 * 2**20
+            collective_id=0, has_side_effects=True, vmem_limit_bytes=53 * 2**20
         ),
         name="sinkhorn",
     )(*ready, pred_feat.T, true_feat.T)

time: 89.5 us -> 86.9 us (0.971)
  Pallas kernels: 85.6 us -> 83.4 us
    pallas_call x1, Pallas kernels: 2.16 us -> 0.72 us  [on_device(): pl.pallas_call(functools.partial(prepare_kernel, ncol, homes), out_shape=...]
    unnamed x2 -> x6, local copies, waits for them, and re-layouts: 2.87 us -> 2.64 us
where the time goes in v5:
time: 86.9 us; the launch traced here: 86.7 us
  Pallas kernels  83.4 us (96%)
  local copies, waits for them, and re-layouts  2.64 us (3%)
    pallas_call x1, Pallas kernels, on_device(): pl.pallas_call(functools.partial(sinkhorn_kernel, (nz, ncol, homes, kmax,...  82.7 us
    unnamed x6, local copies, waits for them, and re-layouts  2.64 us

profile of v5, /device:TPU:1, one launch (start us, length us, event | category | flops | bytes accessed | tf_op | source)
XLA Modules:
  0.0 86.7 jit_solution(9695970900412241048)
XLA Ops:
  0.6 0.0 copy-start
  0.6 0.7 copy-done
  1.3 0.0 copy-start.1
  1.3 0.7 copy-done.1
  2.0 0.7 prepare.1
  2.8 82.7 %sinkhorn.1 = (f32[80,128]{1,0:T(8,128)S(1)}, f32[128,128]{1,0:T(8,128)S(1)}) custom-call(s32[40,128]{1,0:T(8,128)S(1)} %get-tuple-element.6.table, bf16[10,128,64]{2,1,0:T(8,128)(2,1)S(1)} %get-tuple-element.7.onehot_hbm, bf16[64,10240]{1,0:T(8,128)(2,1)} %bitcast.11, bf16[64,16384]{1,0:T(8,128)(2,1)} %bitcast.10), custom_call_target="tpu_custom_call" | custom-call | tf_op jit(solution)/shard_map/sinkhorn/pallas_call | solution.py:403
  85.4 0.6 copy.8
  86.0 0.6 copy.9
Async XLA Ops:
  0.6 0.7 copy-start
  1.3 0.7 copy-start.1
